TPU v7x, 32 devices: a whole 2x2x4 slice. The times are simulated.
32 devices in a mesh: rep: 2 (over y), ep: 4 (over z), tp: 4 (over x, core).
Axes of the slice: x: 2, y: 2, z: 4, core: 2. Of those that a mesh axis runs over, the one named last changes fastest.
Arguments:
- tokens: bfloat16 [256, 4096], P(('rep', 'ep'), 'tp'), parts along dimension 0, may hold values from -200 to 200
- norm_gain: float32 [4096], P('tp'), may hold values from 0.1 to 1.9
- expert_ids: int32 [256, 8], P(('rep', 'ep')), parts along dimension 0, may hold values from 0 to 31, all different within a row; in each aligned block of 32 rows (0 to 31, 32 to 63, ...) at most 16 rows name the same one
- route_weight: float32 [256, 8], P(('rep', 'ep')), parts along dimension 0, may hold values from 0.02 to 0.25
- gate_weight: bfloat16 [32, 4096, 1536], P('ep', None, 'tp'), may hold values from -0.09375 to 0.09375
- up_weight: bfloat16 [32, 4096, 1536], P('ep', None, 'tp'), may hold values from -0.09375 to 0.09375
- down_weight: bfloat16 [32, 1536, 4096], P('ep', 'tp'), may hold values from -0.15625 to 0.15625
Outputs:
- combined: bfloat16 [256, 4096], P(('rep', 'ep'), 'tp'), parts along dimension 0
There are 2 independent parts, one for each index of `rep`. A program takes and returns all parts, laid end to end along the dimension named above; an argument that names none is the same for every part. Nothing has to cross between parts.
Inputs may be any that keep to these rules, and one draw needn't show every extreme that they name: `expert_ids`: in each aligned block of 32 rows (the tokens of one index of ep) no expert is named by more than 16 rows, and in every draw some block names some expert exactly 16 times; a row names 8 different experts.
All inputs are finite; a program needn't handle non-finite values.
Results may differ from a plain program's by a relative error of at most 0.012.
Values may be sent and summed in bfloat16 or wider, within the bound.
A program may use at most 192 MiB of HBM per device.

v0:
```python
import jax
import jax.numpy as jnp
from jax import lax
from jax.sharding import PartitionSpec as P

D = 4096
TOP = 8
EXPERTS = 32
CAP = 16


def entry_slots(route_ids):
    onehot = (route_ids[..., None] == jnp.arange(EXPERTS, dtype=jnp.int32)).astype(jnp.int32)
    before = jnp.cumsum(onehot, axis=-2) - onehot
    return jnp.sum(before * onehot, axis=-1)


def local(tokens, norm_gain, expert_ids, route_weight, gate_weight, up_weight, down_weight):
    ep_count = lax.axis_size("ep")
    local_count = gate_weight.shape[0]
    feature_count = tokens.shape[1]
    tok_count = tokens.shape[0]
    entries = tok_count * TOP
    wide_tok = tokens.astype(jnp.float32)
    squares = lax.psum(jnp.sum(wide_tok * wide_tok, axis=1), "tp")
    inverse = lax.rsqrt(squares / D + 1e-06)
    normed = (wide_tok * inverse[:, None] * norm_gain).astype(jnp.bfloat16)
    flat_ids = expert_ids.reshape(-1)
    slot_ids = entry_slots(flat_ids[None, :])[0]
    position = flat_ids * CAP + slot_ids
    token_row = jnp.arange(entries, dtype=jnp.int32) // TOP
    complete = lax.all_gather(normed, "tp", axis=1, tiled=True)
    columns = complete.shape[1]
    empty = jnp.zeros((EXPERTS * CAP, columns), jnp.bfloat16)
    arrived = lax.all_to_all(
        empty.at[position].set(complete[token_row]).reshape(ep_count, local_count * CAP, columns),
        "ep",
        split_axis=0,
        concat_axis=0,
        tiled=True,
    )
    row_block = arrived.reshape(ep_count, local_count, CAP, D)
    gate_act = jnp.einsum(
        "slcd,ldf->slcf", row_block, gate_weight, preferred_element_type=jnp.float32
    )
    up_act = jnp.einsum("slcd,ldf->slcf", row_block, up_weight, preferred_element_type=jnp.float32)
    hidden = (jax.nn.silu(gate_act) * up_act).astype(jnp.bfloat16)
    partial_value = jnp.einsum(
        "slcf,lfd->slcd", hidden, down_weight, preferred_element_type=jnp.float32
    )
    summed = lax.psum_scatter(
        partial_value.astype(jnp.bfloat16), "tp", scatter_dimension=3, tiled=True
    )
    answer = summed.reshape(ep_count, local_count * CAP, feature_count)
    returned = lax.all_to_all(answer, "ep", split_axis=0, concat_axis=0, tiled=True)
    picked = returned.reshape(EXPERTS * CAP, feature_count)[position].astype(jnp.float32)
    picked = picked.reshape(tok_count, TOP, feature_count)
    combined = jnp.sum(picked * route_weight[:, :, None], axis=1)
    return combined.astype(jnp.bfloat16)


def solution(mesh):
    in_specs = (
        P(("rep", "ep"), "tp"),
        P("tp"),
        P(("rep", "ep"), None),
        P(("rep", "ep"), None),
        P("ep", None, "tp"),
        P("ep", None, "tp"),
        P("ep", "tp", None),
    )
    out_specs = P(("rep", "ep"), "tp")
    return jax.shard_map(local, mesh=mesh, in_specs=in_specs, out_specs=out_specs, check_vma=False)
```

profile of v0, /device:TPU:0, one launch (start us, length us, event | category | flops | bytes accessed | tf_op | source)
XLA Modules:
  0.0 257.7 jit_solution(5871111252474096551)
XLA Ops:
  6.5 0.8 copy.10
  7.3 0.1 eq.27
  7.4 0.6 reduce-window.6
  8.0 0.2 slice_reduce_fusion
  8.3 0.7 broadcast_multiply_fusion
  9.0 0.1 copy.13
  9.2 0.1 mul.55
  9.3 1.0 fusion.42
  10.2 8.3 %psum.7 = f32[32]{0:T(128)S(1)} all-reduce(f32[32]{0:T(128)S(1)} %fusion.42), channel_id=1, replica_groups=mesh['rep'=2,'ep'=4,'tp'=4] {'tp'}, use_global_device_ids=true, to_apply=%region_4.5 | all-reduce | flops 32 | bytes 256 | tf_op jit(solution)/shard_map/psum | solution.py:25
  18.6 0.9 fusion.44
  19.5 5.8 %all_gather.3 = bf16[32,4096]{1,0:T(8,128)(2,1)S(1)} all-gather(bf16[32,1024]{1,0:T(8,128)(2,1)S(1)} %fusion.44), channel_id=1, replica_groups=mesh['rep'=2,'ep'=4,'tp'=4] {'tp'}, dimensions={1}, use_global_device_ids=true | all-gather | bytes 327680 | tf_op jit(solution)/shard_map/all_gather | solution.py:32
  25.3 0.1 broadcast.141
  25.4 0.1 fusion.45
  25.5 12.1 %scatter_custom_fusion = bf16[512,4096]{1,0:T(8,128)(2,1)} fusion(s32[256]{0:T(256)S(1)} %bitcast.73, bf16[32,4096]{1,0:T(8,128)(2,1)S(1)} %all_gather.3, s32[1024]{0:T(1024)S(1)} %pad_clamp_fusion.1, bf16[]{:T(256)} %constant.29.clone.1), kind=kCustom, calls=%fused_computation.13 | custom fusion | bytes 4194306 | tf_op jit(solution)/shard_map/scatter | solution.py:36
  37.6 98.5 %all_to_all.10 = bf16[4,128,4096]{2,1,0:T(8,128)(2,1)S(1)} all-to-all(bf16[4,128,4096]{2,1,0:T(8,128)(2,1)} %bitcast.68), channel_id=1, replica_groups=mesh['rep'=2,'ep'=4,'tp'=4] {'ep'}, dimensions={0} | all-to-all | bytes 8388608 | tf_op jit(solution)/shard_map/all_to_all | solution.py:35
  136.1 2.0 copy-done
  138.1 10.1 %fusion.17 = f32[4,8,16,384]{3,2,0,1:T(8,128)S(1)} fusion(bf16[8,4096,384]{2,1,0:T(8,128)(2,1)} %param.11, bf16[4,8,16,4096]{3,2,1,0:T(8,128)(2,1)S(1)} %bitcast.65), kind=kOutput, calls=%fused_computation.16 | convolution fusion | flops 1610612736 | bytes 30146560 | tf_op jit(solution)/shard_map/slcd,ldf->slcf/dot_general | solution.py:43
  148.2 25.0 %fusion.9 = bf16[4,8,16,4096]{3,2,0,1:T(8,128)(2,1)} fusion(bf16[8,384,4096]{2,1,0:T(8,128)(2,1)} %param.13, bf16[8,4096,384]{2,1,0:T(8,128)(2,1)} %param.12, bf16[4,8,16,4096]{3,2,1,0:T(8,128)(2,1)} %bitcast.66, f32[4,8,16,384]{3,2,0,1:T(8,128)S(1)} %fusion.17), kind=kOutput, calls=%fused_computation.10 | convolution fusion | flops 3224502272 | bytes 59506688 | tf_op jit(solution)/shard_map/slcf,lfd->slcd/dot_general | solution.py:48
  173.2 42.8 %reduce-scatter.2.cloned.1.call-done = bf16[4,8,16,1024]{3,2,0,1:T(8,128)(2,1)} async-done(((bf16[4,8,16,4096]{3,2,0,1:T(8,128)(2,1)}), bf16[4,8,16,1024]{3,2,0,1:T(8,128)(2,1)}) %reduce-scatter.2.cloned.1.call-update) | async-done | bytes 1048592 | tf_op jit(solution)/shard_map/reduce_scatter | solution.py:51
  216.1 2.3 copy.15
  218.4 4.6 %all-to-all-start.1 = ((bf16[4,128,1024]{2,1,0:T(8,128)(2,1)}), bf16[4,128,1024]{2,1,0:T(8,128)(2,1)S(1)}, u32[]{:S(2)}, u32[]{:S(2)}) async-start(bf16[4,128,1024]{2,1,0:T(8,128)(2,1)} %bitcast.20), calls=%async_computation.2 | async-start | bytes 2097152 | tf_op jit(solution)/shard_map/all_to_all | solution.py:55
  223.1 25.6 %all-to-all-done.1 = bf16[4,128,1024]{2,1,0:T(8,128)(2,1)S(1)} async-done(((bf16[4,128,1024]{2,1,0:T(8,128)(2,1)}), bf16[4,128,1024]{2,1,0:T(8,128)(2,1)S(1)}, u32[]{:S(2)}, u32[]{:S(2)}) %all-to-all-start.1) | async-done | bytes 1048608 | tf_op jit(solution)/shard_map/all_to_all | solution.py:55
  248.7 1.2 gather_fusion
  249.9 1.0 fusion.37
  (17 shorter events, 0.3 us)
Async XLA Ops:
  6.5 209.5 %reduce-scatter.2.cloned.1.call-start = ((), (), s32[]{:S(2)}) async-start(), calls=%async_computation.3 | async-start | bytes 5242880 | tf_op jit(solution)/shard_map/reduce_scatter | solution.py:51
  136.1 2.0 copy-start
  173.2 49.8 %copy-start.1 = (f32[32,8]{0,1:T(8,128)S(1)}, f32[32,8]{0,1:T(8,128)}, u32[]{:S(2)}) copy-start(f32[32,8]{0,1:T(8,128)} %param.10) | copy-start | bytes 3076
  218.4 30.3 %all-to-all-start.1 = ((bf16[4,128,1024]{2,1,0:T(8,128)(2,1)}), bf16[4,128,1024]{2,1,0:T(8,128)(2,1)S(1)}, u32[]{:S(2)}, u32[]{:S(2)}) async-start(bf16[4,128,1024]{2,1,0:T(8,128)(2,1)} %bitcast.20), calls=%async_computation.2 | async-start | bytes 2097152 | tf_op jit(solution)/shard_map/all_to_all | solution.py:55
Sparse Core Ops, SparseCore 0:
  173.3 42.6 reduce-scatter.1
where the time goes:
time: 258 us
  blocking collectives  113 us (44%)
  waiting for transfers between devices  68.5 us (27%)
  matrix products  35.1 us (14%)
  local copies, waits for them, and re-layouts  19 us (7%)
  between operations  13.5 us (5%)
  starting transfers between devices  4.6 us (2%)
  other arithmetic  4.37 us (2%)
    all_to_all x1, blocking collectives, local(): lax.all_to_all(empty.at[position].set(complete[token_row]).reshape(ep_cou...  98.5 us
    reduce_scatter x1, waiting for transfers between devices, local(): lax.psum_scatter(partial_value.astype(jnp.bfloat16), 'tp', scatter_dimens...  42.8 us
    all_to_all x1, waiting for transfers between devices, local(): lax.all_to_all(answer, 'ep', split_axis=0, concat_axis=0, tiled=True)  25.6 us
    dot_general x1, matrix products, local(): jnp.einsum('slcf,lfd->slcd', hidden, down_weight, preferred_element_type=...  25 us
    scatter x1, local copies, waits for them, and re-layouts, local(): empty.at[position].set(complete[token_row])  12.1 us
    dot_general x1, matrix products, local(): jnp.einsum('slcd,ldf->slcf', row_block, gate_weight, preferred_element_ty...  10.1 us
    psum x1, blocking collectives, local(): squares = lax.psum(jnp.sum(wide_tok * wide_tok, axis=1), 'tp')  8.34 us
    all_gather x1, blocking collectives, local(): complete = lax.all_gather(normed, 'tp', axis=1, tiled=True)  5.79 us
  transfers between devices with their start and end apart: 2, of which 2 were waited for; matrix products, arithmetic and copies ran while one was open for 0% of the time, Pallas kernels for 0%

commit v1 on v0

v1 whole, which is shorter than its diff:
```python
import functools

import jax
import jax.numpy as jnp
from jax import lax
from jax.experimental import pallas as pl
from jax.experimental.pallas import tpu as pltpu
from jax.sharding import PartitionSpec as P

LANES = 128
MIB = 1 << 20
SLOTS = 5
MESH = pl.DeviceIdType.MESH


def flip(index, mask):
    bit = 1
    while bit <= mask:
        if mask & bit:
            index = index + bit * (1 - 2 * ((index // bit) % 2))
        bit *= 2
    return index


def kernel(n_ep, n_tp, slots, tok_ref, gain_ref, ids_ref, rw_ref, gate_ref, up_ref, down_ref, out_ref,
           x_all, meta, gu, dn, hid, acc, tx, rx, ztx, zrx, wcol,
           gu_sem, dn_sem, ep_send, ep_recv, tp_send, tp_recv, rs_send, rs_recv, z_send, z_recv):
    me, mt = lax.axis_index("ep"), lax.axis_index("tp")
    rows, width = tok_ref.shape
    local, depth, units = gate_ref.shape
    experts = local * n_ep
    total = rows * n_ep
    bits = n_tp.bit_length() - 1
    wide = units % LANES == 0
    fine = n_ep <= 4
    pieces = n_ep if fine else 1

    def gu_copies(e, slot):
        if wide:
            first, second = gu.at[slot, :, pl.ds(0, units)], gu.at[slot, :, pl.ds(units, units)]
        else:
            first, second = gu.at[slot, 0], gu.at[slot, 1]
        return (
            pltpu.make_async_copy(gate_ref.at[e], first, gu_sem.at[slot, 0]),
            pltpu.make_async_copy(up_ref.at[e], second, gu_sem.at[slot, 1]),
        )

    def dn_copy(d):
        start = pl.multiple_of(flip(mt, d) * width, LANES)
        return pltpu.make_async_copy(down_ref.at[:, :, pl.ds(start, width)], dn.at[d], dn_sem.at[d])

    for e in range(slots):
        for copy in gu_copies(e, e):
            copy.start()
    early = [n_tp - 1, n_tp - 2] if slots < local else list(range(n_tp - 1, -1, -1))
    late = [d for d in range(n_tp - 1, -1, -1) if d not in early]
    for d in early:
        dn_copy(d).start()

    barrier = pltpu.get_barrier_semaphore()

    def greet(t, carry):
        pl.semaphore_signal(barrier, inc=1, device_id={"ep": lax.rem(me + t, n_ep)}, device_id_type=MESH)
        return carry

    lax.fori_loop(1, n_ep, greet, 0)
    for b in range(bits):
        pl.semaphore_signal(barrier, inc=1, device_id={"tp": flip(mt, 1 << b)}, device_id_type=MESH)

    raw = tok_ref[...].astype(jnp.float32)
    x_all[mt, me] = (raw * gain_ref[...]).astype(jnp.bfloat16)
    lane = lax.broadcasted_iota(jnp.int32, (rows, LANES), 1)
    table = jnp.zeros((rows, LANES), jnp.float32)
    for k in range(ids_ref.shape[1]):
        table += jnp.where(ids_ref[:, k:k + 1] == lane, rw_ref[:, k:k + 1], 0.0)
    squares = jnp.sum(raw * raw, axis=1, keepdims=True)
    meta[mt, me] = jnp.where(lane == experts, squares, table)

    pl.semaphore_wait(barrier, n_ep - 1 + bits)

    def ep_copies(t, owner):
        to = {"ep": lax.rem(me + t, n_ep)}
        return [
            pltpu.make_async_remote_copy(
                src_ref=ref.at[mt, owner], dst_ref=ref.at[mt, owner], send_sem=ep_send.at[t, i],
                recv_sem=ep_recv.at[t, i], device_id=to, device_id_type=MESH)
            for i, ref in enumerate((x_all, meta))
        ]

    def tp_copies(p, bit, shard, k):
        to = {"tp": flip(mt, bit)}
        made = []
        for i, ref in enumerate((x_all, meta)):
            view = ref.at[shard, lax.rem(me - p + n_ep, n_ep)] if fine else ref.at[shard]
            made.append(pltpu.make_async_remote_copy(
                src_ref=view, dst_ref=view, send_sem=tp_send.at[p, k, i], recv_sem=tp_recv.at[p, k, i],
                device_id=to, device_id_type=MESH))
        return made

    def ep_start(t, carry):
        for copy in ep_copies(t, me):
            copy.start()
        return carry

    def ep_arrive(t, carry):
        for copy in ep_copies(t, lax.rem(me - t + n_ep, n_ep)):
            copy.wait_recv()
        return carry

    def ep_sent(t, carry):
        for copy in ep_copies(t, me):
            copy.wait_send()
        return carry

    masks = {b: [m for m in range(0, n_tp, 2 << b)] for b in range(bits)}
    lax.fori_loop(1, n_ep, ep_start, 0)
    if not fine:
        lax.fori_loop(1, n_ep, ep_arrive, 0)
    for b in range(bits - 1, -1, -1):
        for p in range(pieces):
            if b == bits - 1:
                if fine and p:
                    ep_arrive(p, 0)
            else:
                for m in masks[b + 1]:
                    k = m | (2 << b)
                    for copy in tp_copies(p, 2 << b, flip(mt, k), k):
                        copy.wait_recv()
            for m in masks[b]:
                for copy in tp_copies(p, 1 << b, flip(mt, m), m | (1 << b)):
                    copy.start()
    for p in range(pieces):
        for m in masks[0]:
            for copy in tp_copies(p, 1, flip(mt, m | 1), m | 1):
                copy.wait_recv()

    heads = meta[mt].reshape(total, LANES)
    sums = meta[0].reshape(total, LANES)
    for j in range(1, n_tp):
        sums = sums + meta[j].reshape(total, LANES)
    lane_all = lax.broadcasted_iota(jnp.int32, (total, LANES), 1)
    mean = jnp.sum(jnp.where(lane_all == experts, sums, 0.0), axis=1, keepdims=True) / depth
    inverse = lax.rsqrt(mean + 1e-6)
    wcol[0] = jnp.broadcast_to(inverse, (total, LANES))
    wcol[1] = heads

    def one_expert(e, slot):
        for copy in gu_copies(e, slot):
            copy.wait()
        x = jnp.concatenate([x_all[j].reshape(total, width) for j in range(n_tp)], axis=1)
        if wide:
            both = jnp.dot(x, gu[slot], preferred_element_type=jnp.float32)
            g, u = both[:, :units], both[:, units:]
        else:
            g = jnp.dot(x, gu[slot, 0], preferred_element_type=jnp.float32)
            u = jnp.dot(x, gu[slot, 1], preferred_element_type=jnp.float32)
        scale = wcol[0][:, 0:1]
        lanes = lax.broadcasted_iota(jnp.int32, (total, LANES), 1)
        share = jnp.sum(jnp.where(lanes == me * local + e, wcol[1], 0.0), axis=1, keepdims=True)
        g, u = g * scale, u * scale
        return (g / (1.0 + jnp.exp(-g)) * u * share).astype(jnp.bfloat16)

    if wide:
        def step(e, carry):
            slot = lax.rem(e, slots)
            hid[:, pl.ds(pl.multiple_of(e * units, LANES), units)] = one_expert(e, slot)
            if slots < local:
                @pl.when(e + slots < local)
                def _():
                    for copy in gu_copies(e + slots, slot):
                        copy.start()

                @pl.when(e == local - slots - 1)
                def _():
                    for d in late:
                        dn_copy(d).start()
            return carry

        lax.fori_loop(0, local, step, 0)
    else:
        for e in range(local):
            hid[:, e * units:(e + 1) * units] = one_expert(e, e)

    def rs_copy(p, d):
        b = (d & -d)
        view = lambda ref: ref.at[d, lax.rem(me + 1 + p, n_ep)] if fine else ref.at[d]
        return pltpu.make_async_remote_copy(
            src_ref=view(tx), dst_ref=view(rx), send_sem=rs_send.at[p, d], recv_sem=rs_recv.at[p, d],
            device_id={"tp": flip(mt, b)}, device_id_type=MESH)

    tile = min(width, 256)

    def z_copy(t, slot):
        return pltpu.make_async_remote_copy(
            src_ref=ztx.at[slot], dst_ref=zrx.at[t], send_sem=z_send.at[t], recv_sem=z_recv.at[t],
            device_id={"ep": lax.rem(me + t, n_ep)}, device_id_type=MESH)

    for d in range(n_tp - 1, -1, -1):
        dn_copy(d).wait()

        def column(n, carry, d=d):
            at = pl.ds(pl.multiple_of(n * tile, LANES), tile)
            weights = dn[d, :, :, at].reshape(local * units, tile)
            value = jnp.dot(hid[...], weights, preferred_element_type=jnp.float32)
            acc[:, :, at] = value.reshape(n_ep, rows, tile)
            return carry

        lax.fori_loop(0, width // tile, column, 0)
        sources = []
        b = 1
        while b < n_tp and not d & b:
            sources.append(d | b)
            b *= 2

        def block(s, sources=sources):
            value = acc[s]
            for source in sources:
                value = value + rx[source, s].astype(jnp.float32)
            return value

        if d:
            for p in range(pieces):
                for source in sources:
                    rs_copy(p, source).wait_recv()
                if fine:
                    s = lax.rem(me + 1 + p, n_ep)
                    tx[d, s] = block(s).astype(jnp.bfloat16)
                else:
                    def fill(s, carry, d=d, block=block):
                        tx[d, s] = block(s).astype(jnp.bfloat16)
                        return carry
                    lax.fori_loop(0, n_ep, fill, 0)
                rs_copy(p, d).start()
        else:
            def arrive(p):
                for source in sources:
                    rs_copy(p, source).wait_recv()

            def send(t, carry):
                s = lax.rem(me + t, n_ep)
                ztx[t] = block(s).astype(jnp.bfloat16)
                z_copy(t, t).start()
                return carry

            if fine:
                for t in range(1, n_ep):
                    arrive(t - 1)
                    send(t, 0)
                arrive(n_ep - 1)
            else:
                arrive(0)
                lax.fori_loop(1, n_ep, send, 0)
            acc[me] = block(me)

    def collect(t, carry):
        z_copy(t, t).wait_recv()
        acc[me] += zrx[t].astype(jnp.float32)
        return carry

    lax.fori_loop(1, n_ep, collect, 0)
    out_ref[...] = acc[me].astype(jnp.bfloat16)

    lax.fori_loop(1, n_ep, ep_sent, 0)
    for p in range(pieces):
        for b in range(bits):
            for m in masks[b]:
                for copy in tp_copies(p, 1 << b, flip(mt, m), m | (1 << b)):
                    copy.wait_send()
        for d in range(1, n_tp):
            rs_copy(p, d).wait_send()

    def z_sent(t, carry):
        z_copy(t, t).wait_send()
        return carry

    lax.fori_loop(1, n_ep, z_sent, 0)


def local_part(n_ep, n_tp, tokens, norm_gain, expert_ids, route_weight, gate_weight, up_weight, down_weight):
    rows, width = tokens.shape
    local, depth, units = gate_weight.shape
    total = rows * n_ep
    wide = units % LANES == 0
    slots = min(local, SLOTS) if wide else local
    pieces = n_ep if n_ep <= 4 else 1
    gu_shape = (slots, depth, 2 * units) if wide else (slots, 2, depth, units)
    vmem = pl.BlockSpec(memory_space=pltpu.VMEM)
    hbm = pl.BlockSpec(memory_space=pl.ANY)
    dma = pltpu.SemaphoreType.DMA
    bf16, f32 = jnp.bfloat16, jnp.float32
    return pl.pallas_call(
        functools.partial(kernel, n_ep, n_tp, slots),
        out_shape=jax.ShapeDtypeStruct((rows, width), bf16),
        in_specs=[vmem] * 4 + [hbm] * 3,
        out_specs=vmem,
        scratch_shapes=[
            pltpu.VMEM((n_tp, n_ep, rows, width), bf16),
            pltpu.VMEM((n_tp, n_ep, rows, LANES), f32),
            pltpu.VMEM(gu_shape, bf16),
            pltpu.VMEM((n_tp, local, units, width), bf16),
            pltpu.VMEM((total, local * units), bf16),
            pltpu.VMEM((n_ep, rows, width), f32),
            pltpu.VMEM((n_tp, n_ep, rows, width), bf16),
            pltpu.VMEM((n_tp, n_ep, rows, width), bf16),
            pltpu.VMEM((n_ep, rows, width), bf16),
            pltpu.VMEM((n_ep, rows, width), bf16),
            pltpu.VMEM((2, total, LANES), f32),
            dma((slots, 2)),
            dma((n_tp,)),
            dma((n_ep, 2)),
            dma((n_ep, 2)),
            dma((pieces, n_tp, 2)),
            dma((pieces, n_tp, 2)),
            dma((pieces, n_tp)),
            dma((pieces, n_tp)),
            dma((n_ep,)),
            dma((n_ep,)),
        ],
        compiler_params=pltpu.CompilerParams(
            collective_id=0, has_side_effects=True, vmem_limit_bytes=62 * MIB
        ),
        cost_estimate=pl.CostEstimate(
            flops=6 * total * local * depth * units,
            bytes_accessed=6 * local * depth * units,
            transcendentals=total * local * units,
        ),
    )(tokens, norm_gain.reshape(1, width), expert_ids, route_weight, gate_weight, up_weight, down_weight)


def solution(mesh):
    in_specs = (
        P(("rep", "ep"), "tp"),
        P("tp"),
        P(("rep", "ep"), None),
        P(("rep", "ep"), None),
        P("ep", None, "tp"),
        P("ep", None, "tp"),
        P("ep", "tp", None),
    )
    run = functools.partial(local_part, mesh.shape["ep"], mesh.shape["tp"])
    return jax.shard_map(
        run, mesh=mesh, in_specs=in_specs, out_specs=P(("rep", "ep"), "tp"), check_vma=False)
```

time: 258 us -> 49.7 us (0.19)
  blocking collectives: 113 us -> 0 us
  waiting for transfers between devices: 68.5 us -> 0 us
  Pallas kernels: 0 us -> 45.2 us
  matrix products: 35.1 us -> 0 us
  local copies, waits for them, and re-layouts: 19 us -> 4.2 us
  between operations: 13.5 us -> 0.01 us
  starting transfers between devices: 4.6 us -> 0 us
  other arithmetic: 4.37 us -> 0 us
    all_to_all x1 -> x0, blocking collectives: 98.5 us -> none  [local(): lax.all_to_all(empty.at[position].set(complete[token_row]).reshape(ep_cou...]
    pallas_call x0 -> x1, Pallas kernels: none -> 45.2 us  [local_part(): pl.pallas_call(functools.partial(kernel, n_ep, n_tp, slots), out_shape=ja...]
    reduce_scatter x1 -> x0, waiting for transfers between devices: 42.8 us -> none  [local(): lax.psum_scatter(partial_value.astype(jnp.bfloat16), 'tp', scatter_dimens...]
    dot_general x2 -> x0, matrix products: 35.1 us -> none  [the longest x1 25 us: local(): jnp.einsum('slcf,lfd->slcd', hidden, down_weight, preferred_element_type=...]
    all_to_all x1 -> x0, waiting for transfers between devices: 25.6 us -> none  [local(): lax.all_to_all(answer, 'ep', split_axis=0, concat_axis=0, tiled=True)]
    scatter x1 -> x0, local copies, waits for them, and re-layouts: 12.1 us -> none  [local(): empty.at[position].set(complete[token_row])]
    psum x1 -> x0, blocking collectives: 8.34 us -> none  [local(): squares = lax.psum(jnp.sum(wide_tok * wide_tok, axis=1), 'tp')]
    all_gather x1 -> x0, blocking collectives: 5.79 us -> none  [local(): complete = lax.all_gather(normed, 'tp', axis=1, tiled=True)]
  transfers between devices with their start and end apart: 2 -> 0, of which waited for: 2 -> 0; matrix products, arithmetic and copies ran while one was open for 0% -> 0% of each run, Pallas kernels for 0% -> 0%
where the time goes in v1:
time: 49.7 us; the launch traced here: 49.4 us
  Pallas kernels  45.2 us (91%)
  local copies, waits for them, and re-layouts  4.2 us (8%)
    pallas_call x1, Pallas kernels, local_part(): pl.pallas_call(functools.partial(kernel, n_ep, n_tp, slots), out_shape=ja...  45.2 us
    unnamed x3, local copies, waits for them, and re-layouts  4.2 us

profile of v1, /device:TPU:0, one launch (start us, length us, event | category | flops | bytes accessed | tf_op | source)
XLA Modules:
  0.0 49.4 jit_solution(9345374697762180254)
XLA Ops:
  0.0 1.4 %copy.8.ids_ref = s32[32,8]{1,0:T(8,128)} copy(s32[32,8]{0,1:T(8,128)} %param.9) | data formatting | bytes 2048 | tf_op args[2]
  1.4 1.4 %copy.9.rw_ref = f32[32,8]{1,0:T(8,128)} copy(f32[32,8]{0,1:T(8,128)} %param.10) | data formatting | bytes 2048 | tf_op args[3]
  2.7 45.2 %shard_map.73 = bf16[32,1024]{1,0:T(8,128)(2,1)} custom-call(bf16[32,1024]{1,0:T(8,128)(2,1)} %tok_ref.1, f32[1,1024]{1,0:T(1,128)} %bitcast.1, s32[32,8]{1,0:T(8,128)} %copy.8.ids_ref, f32[32,8]{1,0:T(8,128)} %copy.9.rw_ref, bf16[8,4096,384]{2,1,0:T(8,128)(2,1)} %gate_ref.1, bf16[8,4096,384]{2,1,0:T(8,128)(2,1)} %up_ref.1, bf16[8,384,4096]{2,1,0:T(8,128)(2,1)} %down_ref.1), custom_call_target="tpu_custom_call" | custom-call | flops 9663676416 | bytes 75497472 | tf_op jit(solution)/shard_map/pallas_call | solution.py:291
  47.9 1.5 %copy.11 = bf16[32,1024]{1,0:T(8,128)(2,1)} copy(bf16[32,1024]{1,0:T(8,128)(2,1)} %shard_map.73) | data formatting | bytes 131072

commit v2 on v1

--- a/solution.py
+++ b/solution.py
@@ -10,6 +10,7 @@
 LANES = 128
 MIB = 1 << 20
 SLOTS = 5
+HALVES = 2
 MESH = pl.DeviceIdType.MESH
 
 
@@ -52,7 +53,7 @@
     for e in range(slots):
         for copy in gu_copies(e, e):
             copy.start()
-    early = [n_tp - 1, n_tp - 2] if slots < local else list(range(n_tp - 1, -1, -1))
+    early = list(range(n_tp - 1, 0, -1)) if slots < local else list(range(n_tp - 1, -1, -1))
     late = [d for d in range(n_tp - 1, -1, -1) if d not in early]
     for d in early:
         dn_copy(d).start()
@@ -181,84 +182,94 @@
         for e in range(local):
             hid[:, e * units:(e + 1) * units] = one_expert(e, e)
 
-    def rs_copy(p, d):
-        b = (d & -d)
-        view = lambda ref: ref.at[d, lax.rem(me + 1 + p, n_ep)] if fine else ref.at[d]
+    half = width // HALVES
+    tile = min(half, 256)
+
+    def rs_copy(p, d, h):
+        view = lambda ref: ref.at[h, d, lax.rem(me + 1 + p, n_ep)] if fine else ref.at[h, d]
         return pltpu.make_async_remote_copy(
-            src_ref=view(tx), dst_ref=view(rx), send_sem=rs_send.at[p, d], recv_sem=rs_recv.at[p, d],
-            device_id={"tp": flip(mt, b)}, device_id_type=MESH)
-
-    tile = min(width, 256)
-
-    def z_copy(t, slot):
+            src_ref=view(tx), dst_ref=view(rx), send_sem=rs_send.at[p, d, h], recv_sem=rs_recv.at[p, d, h],
+            device_id={"tp": flip(mt, d & -d)}, device_id_type=MESH)
+
+    def z_copy(t, h):
         return pltpu.make_async_remote_copy(
-            src_ref=ztx.at[slot], dst_ref=zrx.at[t], send_sem=z_send.at[t], recv_sem=z_recv.at[t],
+            src_ref=ztx.at[h, t], dst_ref=zrx.at[h, t], send_sem=z_send.at[t, h], recv_sem=z_recv.at[t, h],
             device_id={"ep": lax.rem(me + t, n_ep)}, device_id_type=MESH)
 
-    for d in range(n_tp - 1, -1, -1):
-        dn_copy(d).wait()
-
-        def column(n, carry, d=d):
+    def sources_of(d):
+        return [d | (1 << b) for b in range(bits) if not d & ((2 << b) - 1)]
+
+    def block(s, d, h):
+        value = acc[h if d == 0 else HALVES, s]
+        for source in sources_of(d):
+            value = value + rx[h, source, s].astype(jnp.float32)
+        return value
+
+    def arrive(p, d, h):
+        for source in sources_of(d):
+            rs_copy(p, source, h).wait_recv()
+
+    def multiply(d, h):
+        if h == 0:
+            dn_copy(d).wait()
+        target = h if d == 0 else HALVES
+
+        def column(n, carry):
             at = pl.ds(pl.multiple_of(n * tile, LANES), tile)
-            weights = dn[d, :, :, at].reshape(local * units, tile)
-            value = jnp.dot(hid[...], weights, preferred_element_type=jnp.float32)
-            acc[:, :, at] = value.reshape(n_ep, rows, tile)
+            weights = dn[d, :, :, pl.ds(pl.multiple_of(h * half + n * tile, LANES), tile)]
+            value = jnp.dot(hid[...], weights.reshape(local * units, tile), preferred_element_type=jnp.float32)
+            acc[target, :, :, at] = value.reshape(n_ep, rows, tile)
             return carry
 
-        lax.fori_loop(0, width // tile, column, 0)
-        sources = []
-        b = 1
-        while b < n_tp and not d & b:
-            sources.append(d | b)
-            b *= 2
-
-        def block(s, sources=sources):
-            value = acc[s]
-            for source in sources:
-                value = value + rx[source, s].astype(jnp.float32)
-            return value
-
-        if d:
-            for p in range(pieces):
-                for source in sources:
-                    rs_copy(p, source).wait_recv()
-                if fine:
-                    s = lax.rem(me + 1 + p, n_ep)
-                    tx[d, s] = block(s).astype(jnp.bfloat16)
-                else:
-                    def fill(s, carry, d=d, block=block):
-                        tx[d, s] = block(s).astype(jnp.bfloat16)
-                        return carry
-                    lax.fori_loop(0, n_ep, fill, 0)
-                rs_copy(p, d).start()
+        lax.fori_loop(0, half // tile, column, 0)
+
+    def pass_on(d, h):
+        for p in range(pieces):
+            arrive(p, d, h)
+            if fine:
+                s = lax.rem(me + 1 + p, n_ep)
+                tx[h, d, s] = block(s, d, h).astype(jnp.bfloat16)
+            else:
+                def fill(s, carry):
+                    tx[h, d, s] = block(s, d, h).astype(jnp.bfloat16)
+                    return carry
+                lax.fori_loop(0, n_ep, fill, 0)
+            rs_copy(p, d, h).start()
+
+    def finish(h):
+        def send(t, carry):
+            ztx[h, t] = block(lax.rem(me + t, n_ep), 0, h).astype(jnp.bfloat16)
+            z_copy(t, h).start()
+            return carry
+
+        if fine:
+            for t in range(1, n_ep):
+                arrive(t - 1, 0, h)
+                send(t, 0)
+            arrive(n_ep - 1, 0, h)
         else:
-            def arrive(p):
-                for source in sources:
-                    rs_copy(p, source).wait_recv()
-
-            def send(t, carry):
-                s = lax.rem(me + t, n_ep)
-                ztx[t] = block(s).astype(jnp.bfloat16)
-                z_copy(t, t).start()
-                return carry
-
-            if fine:
-                for t in range(1, n_ep):
-                    arrive(t - 1)
-                    send(t, 0)
-                arrive(n_ep - 1)
-            else:
-                arrive(0)
-                lax.fori_loop(1, n_ep, send, 0)
-            acc[me] = block(me)
+            arrive(0, 0, h)
+            lax.fori_loop(1, n_ep, send, 0)
+        acc[h, me] = block(me, 0, h)
+
+    for h in range(HALVES):
+        for d in range(n_tp - 1, -1, -1):
+            multiply(d, h)
+            if d:
+                pass_on(d, h)
+            if h and d == n_tp // 2:
+                finish(h - 1)
+    finish(HALVES - 1)
 
     def collect(t, carry):
-        z_copy(t, t).wait_recv()
-        acc[me] += zrx[t].astype(jnp.float32)
+        for h in range(HALVES):
+            z_copy(t, h).wait_recv()
+            acc[h, me] += zrx[h, t].astype(jnp.float32)
         return carry
 
     lax.fori_loop(1, n_ep, collect, 0)
-    out_ref[...] = acc[me].astype(jnp.bfloat16)
+    for h in range(HALVES):
+        out_ref[:, h * half:(h + 1) * half] = acc[h, me].astype(jnp.bfloat16)
 
     lax.fori_loop(1, n_ep, ep_sent, 0)
     for p in range(pieces):
@@ -267,10 +278,12 @@
                 for copy in tp_copies(p, 1 << b, flip(mt, m), m | (1 << b)):
                     copy.wait_send()
         for d in range(1, n_tp):
-            rs_copy(p, d).wait_send()
+            for h in range(HALVES):
+                rs_copy(p, d, h).wait_send()
 
     def z_sent(t, carry):
-        z_copy(t, t).wait_send()
+        for h in range(HALVES):
+            z_copy(t, h).wait_send()
         return carry
 
     lax.fori_loop(1, n_ep, z_sent, 0)
@@ -283,6 +296,7 @@
     wide = units % LANES == 0
     slots = min(local, SLOTS) if wide else local
     pieces = n_ep if n_ep <= 4 else 1
+    half = width // HALVES
     gu_shape = (slots, depth, 2 * units) if wide else (slots, 2, depth, units)
     vmem = pl.BlockSpec(memory_space=pltpu.VMEM)
     hbm = pl.BlockSpec(memory_space=pl.ANY)
@@ -299,11 +313,11 @@
             pltpu.VMEM(gu_shape, bf16),
             pltpu.VMEM((n_tp, local, units, width), bf16),
             pltpu.VMEM((total, local * units), bf16),
-            pltpu.VMEM((n_ep, rows, width), f32),
-            pltpu.VMEM((n_tp, n_ep, rows, width), bf16),
-            pltpu.VMEM((n_tp, n_ep, rows, width), bf16),
-            pltpu.VMEM((n_ep, rows, width), bf16),
-            pltpu.VMEM((n_ep, rows, width), bf16),
+            pltpu.VMEM((HALVES + 1, n_ep, rows, half), f32),
+            pltpu.VMEM((HALVES, n_tp, n_ep, rows, half), bf16),
+            pltpu.VMEM((HALVES, n_tp, n_ep, rows, half), bf16),
+            pltpu.VMEM((HALVES, n_ep, rows, half), bf16),
+            pltpu.VMEM((HALVES, n_ep, rows, half), bf16),
             pltpu.VMEM((2, total, LANES), f32),
             dma((slots, 2)),
             dma((n_tp,)),
@@ -311,10 +325,10 @@
             dma((n_ep, 2)),
             dma((pieces, n_tp, 2)),
             dma((pieces, n_tp, 2)),
-            dma((pieces, n_tp)),
-            dma((pieces, n_tp)),
-            dma((n_ep,)),
-            dma((n_ep,)),
+            dma((pieces, n_tp, HALVES)),
+            dma((pieces, n_tp, HALVES)),
+            dma((n_ep, HALVES)),
+            dma((n_ep, HALVES)),
         ],
         compiler_params=pltpu.CompilerParams(
             collective_id=0, has_side_effects=True, vmem_limit_bytes=62 * MIB

time: 49.7 us -> 48 us (0.966)
  Pallas kernels: 45.2 us -> 43.6 us
    pallas_call x1, Pallas kernels: 45.2 us -> 43.6 us  [local_part(): pl.pallas_call(functools.partial(kernel, n_ep, n_tp, slots), out_shape=ja...]
where the time goes in v2:
time: 48 us; the launch traced here: 47.8 us
  Pallas kernels  43.6 us (91%)
  local copies, waits for them, and re-layouts  4.2 us (9%)
    pallas_call x1, Pallas kernels, local_part(): pl.pallas_call(functools.partial(kernel, n_ep, n_tp, slots), out_shape=ja...  43.6 us
    unnamed x3, local copies, waits for them, and re-layouts  4.2 us

profile of v2, /device:TPU:0, one launch (start us, length us, event | category | flops | bytes accessed | tf_op | source)
XLA Modules:
  0.0 47.8 jit_solution(9947593483423400275)
XLA Ops:
  0.0 1.4 %copy.8.ids_ref = s32[32,8]{1,0:T(8,128)} copy(s32[32,8]{0,1:T(8,128)} %param.9) | data formatting | bytes 2048 | tf_op args[2]
  1.4 1.4 %copy.9.rw_ref = f32[32,8]{1,0:T(8,128)} copy(f32[32,8]{0,1:T(8,128)} %param.10) | data formatting | bytes 2048 | tf_op args[3]
  2.7 43.6 %shard_map.73 = bf16[32,1024]{1,0:T(8,128)(2,1)} custom-call(bf16[32,1024]{1,0:T(8,128)(2,1)} %tok_ref.1, f32[1,1024]{1,0:T(1,128)} %bitcast.1, s32[32,8]{1,0:T(8,128)} %copy.8.ids_ref, f32[32,8]{1,0:T(8,128)} %copy.9.rw_ref, bf16[8,4096,384]{2,1,0:T(8,128)(2,1)} %gate_ref.1, bf16[8,4096,384]{2,1,0:T(8,128)(2,1)} %up_ref.1, bf16[8,384,4096]{2,1,0:T(8,128)(2,1)} %down_ref.1), custom_call_target="tpu_custom_call" | custom-call | flops 9663676416 | bytes 75497472 | tf_op jit(solution)/shard_map/pallas_call | solution.py:305
  46.3 1.5 %copy.11 = bf16[32,1024]{1,0:T(8,128)(2,1)} copy(bf16[32,1024]{1,0:T(8,128)(2,1)} %shard_map.73) | data formatting | bytes 131072
